TPU v7x, 512 devices: a whole 4x8x8 slice. The times are simulated.
512 devices in a mesh: seq: 32 (over x, z), tp: 16 (over y, core).
Axes of the slice: x: 4, y: 8, z: 8, core: 2. Of those that a mesh axis runs over, the one named last changes fastest.
Arguments:
- tokens: bfloat16 [32, 192, 3072], P('seq', None, 'tp'), may hold values from -17 to 17
- spatial_query: bfloat16 [32, 192, 2048], P('seq', None, 'tp'), may hold values from -4 to 4
- spatial_key: bfloat16 [32, 192, 2048], P('seq', None, 'tp'), may hold values from -4 to 4
- spatial_value: bfloat16 [32, 192, 2048], P('seq', None, 'tp'), may hold values from -5 to 5
- spatial_gain: float32 [2, 16, 128], P(None, 'tp'), may hold values from 0.5 to 4.5
- spatial_proj: bfloat16 [2048, 3072], P('tp'), may hold values from -0.5 to 0.5
- spatial_gate: float32 [3072], replicated, may hold values from -3 to 3
- temporal_shift: float32 [3072], replicated, may hold values from -2.5 to 2.5
- temporal_scale: float32 [3072], replicated, may hold values from -2.5 to 2.5
- temporal_weights: bfloat16 [3072, 16, 3, 128], P(None, 'tp'), may hold values from -0.073973 to 0.073973
- temporal_gain: float32 [2, 16, 128], P(None, 'tp'), may hold values from 0.5 to 4.5
- temporal_proj: bfloat16 [2048, 3072], P('tp'), may hold values from -0.5 to 0.5
- temporal_gate: float32 [3072], replicated, may hold values from -3 to 3
Outputs:
- block_output: bfloat16 [32, 192, 3072], P(None, 'seq', 'tp')
All inputs are finite; a program needn't handle non-finite values.
Results may differ from a plain program's by a relative error of at most 0.029.
Values may be sent and summed in bfloat16 or wider, within the bound.
A program may use at most 64 MiB of HBM per device.

v0:
```python
import jax
import jax.numpy as jnp
from jax import lax
from jax.sharding import PartitionSpec as P

NORM_EPS = 1e-06


def head_norm(values, gain):
    square_mean = jnp.mean(values * values, axis=-1, keepdims=True)
    return (values * lax.rsqrt(square_mean + NORM_EPS) * gain).astype(jnp.bfloat16)


def modulated_norm(rows, scale_vec, shift_vec):
    centre = rows - jnp.mean(rows, axis=-1, keepdims=True)
    variance = jnp.mean(centre * centre, axis=-1, keepdims=True)
    return (centre * lax.rsqrt(variance + NORM_EPS) * (1.0 + scale_vec) + shift_vec).astype(
        jnp.bfloat16
    )


def temporal_inputs(full_rows, temporal_shift, temporal_scale, temporal_weights, temporal_gain):
    leading = full_rows.shape[:2]
    model_width, head_count, triple, head_size = temporal_weights.shape
    normed = modulated_norm(full_rows.astype(jnp.float32), temporal_scale, temporal_shift)
    projected = jnp.dot(
        normed.reshape(-1, model_width),
        temporal_weights.reshape(model_width, -1),
        preferred_element_type=jnp.float32,
    )
    projected = projected.reshape(leading + (head_count, triple, head_size))
    query_part = head_norm(projected[:, :, :, 0, :], temporal_gain[0])
    key_part = head_norm(projected[:, :, :, 1, :], temporal_gain[1])
    value_part = projected[:, :, :, 2, :].astype(jnp.bfloat16)
    return (query_part, key_part, value_part)


def spatial_rows(tokens, first_terms, spatial_gate, gather_tokens, sum_terms):
    token_rows = gather_tokens(tokens)
    summed = sum_terms(first_terms)
    return (token_rows.astype(jnp.float32) + spatial_gate * summed).astype(jnp.bfloat16)


def local(
    tokens,
    spatial_query,
    spatial_key,
    spatial_value,
    spatial_gain,
    spatial_proj,
    spatial_gate,
    temporal_shift,
    temporal_scale,
    temporal_weights,
    temporal_gain,
    temporal_proj,
    temporal_gate,
):
    frame_count, place_count, slice_width = tokens.shape
    head_count = spatial_gain.shape[1]
    head_size = spatial_gain.shape[2]
    model_width = spatial_proj.shape[1]
    score_scale = head_size ** (-0.5)
    tensor_rank = lax.axis_index("tp")
    head_shape = (frame_count, place_count, head_count, head_size)
    query_rows = head_norm(spatial_query.astype(jnp.float32).reshape(head_shape), spatial_gain[0])
    key_rows = head_norm(spatial_key.astype(jnp.float32).reshape(head_shape), spatial_gain[1])
    scores = (
        jnp.einsum("fshd,fthd->fhst", query_rows, key_rows, preferred_element_type=jnp.float32)
        * score_scale
    )
    attention = jax.nn.softmax(scores, axis=-1).astype(jnp.bfloat16)
    spatial_heads = jnp.einsum(
        "fhst,fthd->fshd",
        attention,
        spatial_value.reshape(head_shape),
        preferred_element_type=jnp.float32,
    ).astype(jnp.bfloat16)
    row_count = frame_count * place_count
    first_terms = jnp.dot(
        spatial_heads.reshape(row_count, head_count * head_size),
        spatial_proj,
        preferred_element_type=jnp.float32,
    ).reshape(frame_count, place_count, model_width)
    gate_second = lax.dynamic_slice_in_dim(temporal_gate, tensor_rank * slice_width, slice_width)
    mid_rows = spatial_rows(
        tokens,
        first_terms,
        spatial_gate,
        lambda rows: lax.all_gather(rows, "tp", axis=2, tiled=True),
        lambda terms: lax.psum(terms.astype(jnp.bfloat16), "tp").astype(jnp.float32),
    )
    full_rows = lax.all_to_all(mid_rows, "seq", split_axis=1, concat_axis=0, tiled=True)
    residual_space = lax.dynamic_slice_in_dim(full_rows, tensor_rank * slice_width, slice_width, 2)
    query_time, key_time, value_time = temporal_inputs(
        full_rows, temporal_shift, temporal_scale, temporal_weights, temporal_gain
    )
    scores_time = (
        jnp.einsum("fshd,gshd->shfg", query_time, key_time, preferred_element_type=jnp.float32)
        * score_scale
    )
    attention_time = jax.nn.softmax(scores_time, axis=-1).astype(jnp.bfloat16)
    temporal_heads = jnp.einsum(
        "shfg,gshd->fshd", attention_time, value_time, preferred_element_type=jnp.float32
    ).astype(jnp.bfloat16)
    frames_all = temporal_heads.shape[0]
    places_dev = temporal_heads.shape[1]
    second_terms = jnp.dot(
        temporal_heads.reshape(frames_all * places_dev, head_count * head_size),
        temporal_proj,
        preferred_element_type=jnp.float32,
    ).reshape(frames_all, places_dev, model_width)
    second_share = lax.psum_scatter(
        second_terms.astype(jnp.bfloat16), "tp", scatter_dimension=2, tiled=True
    ).astype(jnp.float32)
    return (residual_space.astype(jnp.float32) + gate_second * second_share).astype(jnp.bfloat16)


def solution(mesh):
    placed = (
        P("seq", None, "tp"),
        P("seq", None, "tp"),
        P("seq", None, "tp"),
        P("seq", None, "tp"),
        P(None, "tp", None),
        P("tp", None),
        P(),
        P(),
        P(),
        P(None, "tp", None, None),
        P(None, "tp", None),
        P("tp", None),
        P(),
    )
    return jax.shard_map(
        local, mesh=mesh, in_specs=placed, out_specs=P(None, "seq", "tp"), check_vma=False
    )
```

profile of v0, /device:TPU:1, one launch (start us, length us, event | category | flops | bytes accessed | tf_op | source)
XLA Modules:
  0.0 327.8 jit_solution(7229542557471194334)
XLA Ops:
  6.5 0.0 copy-start
  6.5 0.0 all-gather.2.cloned.1.call-start
  6.5 1.8 copy.29
  8.3 0.0 all-gather.2.cloned.1.call-update
  8.4 0.0 all-reduce.2.cloned.1.call-start
  8.4 0.9 fusion.25
  9.3 0.9 fusion.29
  10.3 0.7 slice_bitcast_fusion.3
  10.9 1.1 fusion.61
  12.1 0.1 fusion.21
  12.1 0.0 copy-done
  12.1 2.5 fusion.1
  14.6 0.0 all-reduce.2.cloned.1.call-update
  14.6 0.0 copy-start.4
  14.7 44.3 %all-gather.2.cloned.1.call-done = bf16[1,192,3072]{1,0,2:T(2,128)(2,1)} async-done(((bf16[1,192,192]{1,0,2:T(2,128)(2,1)}), bf16[1,192,3072]{1,0,2:T(2,128)(2,1)}) %all-gather.2.cloned.1.call-update) | async-done | bytes 1179664 | tf_op jit(solution)/shard_map/all_gather | solution.py:90
  58.9 7.2 %copy.30 = bf16[1,192,3072]{2,1,0:T(8,128)(2,1)S(1)} copy(bf16[1,192,3072]{1,0,2:T(2,128)(2,1)} %all-gather.2.cloned.1.call-done) | data formatting | bytes 2359296 | tf_op jit(solution)/shard_map/all_gather | solution.py:90
  66.2 110.8 %all-reduce.2.cloned.1.call-done = bf16[1,192,3072]{2,1,0:T(8,128)(2,1)} async-done(((bf16[1,192,3072]{2,1,0:T(8,128)(2,1)}), bf16[1,192,3072]{2,1,0:T(8,128)(2,1)}) %all-reduce.2.cloned.1.call-update) | async-done | bytes 1179664 | tf_op jit(solution)/shard_map/psum | solution.py:91
  177.0 0.0 copy-done.4
  177.0 1.7 add_convert_fusion
  178.7 1.8 copy.56
  180.5 0.5 broadcast.246
  181.0 8.7 %reduce.20 = bf16[192,3072]{1,0:T(8,128)(2,1)} reduce(bf16[192,1,3072]{2,1,0:T(2,128)(2,1)S(1)} %bitcast.120, bf16[]{:T(256)} %broadcast.246), dimensions={1}, to_apply=%bitcast.115.reduce_sub_computation | reduce | bytes 2359298
  189.8 0.0 copy-start.1
  189.8 2.8 reshape.443
  192.6 10.2 %all-to-all-start = ((bf16[32,2,9216]{2,1,0:T(2,128)(2,1)}), bf16[32,2,9216]{2,1,0:T(2,128)(2,1)}, u32[]{:S(2)}, u32[]{:S(2)}) async-start(bf16[32,2,9216]{2,1,0:T(2,128)(2,1)} %reshape.443), calls=%async_computation | async-start | bytes 2359296 | tf_op jit(solution)/shard_map/all_to_all | solution.py:93
  202.8 0.0 copy-start.5
  202.8 0.0 copy-start.3
  202.8 0.0 reduce-scatter.4.cloned.1.call-start
  202.8 0.0 copy-done.1
  202.9 2.4 copy.34
  205.3 0.0 copy-done.5
  205.3 0.0 copy-done.3
  205.3 25.0 %all-to-all-done = bf16[32,2,9216]{2,1,0:T(2,128)(2,1)} async-done(((bf16[32,2,9216]{2,1,0:T(2,128)(2,1)}), bf16[32,2,9216]{2,1,0:T(2,128)(2,1)}, u32[]{:S(2)}, u32[]{:S(2)}) %all-to-all-start) | async-done | bytes 1179680 | tf_op jit(solution)/shard_map/all_to_all | solution.py:93
  230.3 4.3 %reshape.444 = bf16[192,1,3072]{2,1,0:T(2,128)(2,1)S(1)} reshape(bf16[32,2,9216]{2,1,0:T(2,128)(2,1)} %all-to-all-done) | data formatting | bytes 2359296
  234.6 0.0 copy-start.2
  234.6 0.4 convert_reduce_fusion
  235.0 0.5 fusion.4
  235.5 0.0 copy-done.2
  235.5 1.8 fusion.7
  237.3 2.4 convert_element_type.170
  239.8 3.4 %fusion.11 = f32[32,6,1,3,128]{4,0,3,1,2:T(8,128)S(1)} fusion(bf16[3072,1,3,128]{0,3,2,1:T(8,128)(2,1)} %copy.34, bf16[32,6,3072,1]{2,1,0,3:T(8,128)(2,1)} %bitcast.121), kind=kOutput, calls=%fused_computation.16 | convolution fusion | flops 452984832 | bytes 3833856 | tf_op jit(solution)/shard_map/dot_general | solution.py:26
  243.1 0.1 multiply_reduce_fusion.1
  243.3 0.2 convolution_multiply_fusion.1
  243.6 2.8 convolution_convert_fusion
  246.4 6.7 %copy.41 = bf16[32,6,3072]{0,1,2:T(8,128)(2,1)} copy(bf16[32,6,3072]{2,0,1:T(8,128)(2,1)} %convolution_convert_fusion) | data formatting | bytes 2359296
  253.0 8.0 %reshape.440 = bf16[3072,192]{1,0:T(8,128)(2,1)} reshape(bf16[3072,6,32]{2,1,0:T(8,128)(2,1)} %bitcast.119) | data formatting | bytes 2359296
  261.0 0.0 reduce-scatter.4.cloned.1.call-update
  261.1 0.8 dynamic_slice.7
  261.8 7.8 %bitcast_reduce_fusion = bf16[192,3072]{1,0:T(8,128)(2,1)} fusion(bf16[192,1,3072]{2,1,0:T(2,128)(2,1)S(1)} %reshape.444), kind=kLoop, calls=%fused_computation.84 | loop fusion | bytes 2359296 | tf_op jit(solution)/shard_map/all_to_all | solution.py:93
  269.6 1.5 all_to_all.10
  271.1 0.1 constant_dynamic-slice_fusion
  271.3 48.0 %reduce-scatter.4.cloned.1.call-done = bf16[192,192]{1,0:T(8,128)(2,1)} async-done(((bf16[3072,192]{1,0:T(8,128)(2,1)}), bf16[192,192]{1,0:T(8,128)(2,1)}) %reduce-scatter.4.cloned.1.call-update) | async-done | bytes 73744
  319.2 1.1 reshape.441
  320.4 0.2 copy.42
  320.6 0.7 fusion.20
  (8 shorter events, 0.1 us)
Async XLA Ops:
  6.5 5.6 %copy-start = (bf16[128,3072]{1,0:T(8,128)(2,1)S(1)}, bf16[128,3072]{1,0:T(8,128)(2,1)}, u32[]{:S(2)}) copy-start(bf16[128,3072]{1,0:T(8,128)(2,1)} %param.18) | copy-start | bytes 2359300
  6.5 52.4 %all-gather.2.cloned.1.call-start = ((), (), s32[]{:S(2)}) async-start(), calls=%async_computation.2 | async-start | bytes 3342336 | tf_op jit(solution)/shard_map/all_gather | solution.py:90
  8.4 168.6 %all-reduce.2.cloned.1.call-start = ((), (), s32[]{:S(2)}) async-start(), calls=%async_computation.3 | async-start | bytes 2359296 | tf_op jit(solution)/shard_map/psum | solution.py:91
  14.6 162.3 %copy-start.4 = (f32[3072]{0:T(1024)S(1)}, f32[3072]{0:T(1024)}, u32[]{:S(2)}) copy-start(f32[3072]{0:T(1024)} %param.19) | copy-start | bytes 36868
  189.8 13.1 %copy-start.1 = (bf16[3072,1,3,128]{3,0,2,1:T(8,128)(2,1)S(1)}, bf16[3072,1,3,128]{3,0,2,1:T(8,128)(2,1)}, u32[]{:S(2)}) copy-start(bf16[3072,1,3,128]{3,0,2,1:T(8,128)(2,1)} %param.22) | copy-start | bytes 7077892
  192.6 37.7 %all-to-all-start = ((bf16[32,2,9216]{2,1,0:T(2,128)(2,1)}), bf16[32,2,9216]{2,1,0:T(2,128)(2,1)}, u32[]{:S(2)}, u32[]{:S(2)}) async-start(bf16[32,2,9216]{2,1,0:T(2,128)(2,1)} %reshape.443), calls=%async_computation | async-start | bytes 2359296 | tf_op jit(solution)/shard_map/all_to_all | solution.py:93
  202.8 2.5 copy-start.5
  202.8 2.5 copy-start.3
  202.8 116.4 %reduce-scatter.4.cloned.1.call-start = ((), (), s32[]{:S(2)}) async-start(), calls=%async_computation.4 | async-start | bytes 1671168
  234.6 0.9 copy-start.2
Sparse Core Ops, SparseCore 0:
  9.5 49.3 all-gather.1
  61.3 115.6 all-reduce.1
  261.2 58.0 reduce-scatter.3
where the time goes:
time: 330 us; the launch traced here: 328 us
  waiting for transfers between devices  228 us (69%)
  local copies, waits for them, and re-layouts  50.2 us (15%)
  other arithmetic  15.9 us (5%)
  between operations  13.3 us (4%)
  starting transfers between devices  10.3 us (3%)
  matrix products  10 us (3%)
    psum x1, waiting for transfers between devices, local(): lax.psum(terms.astype(jnp.bfloat16), 'tp').astype(jnp.float32)  111 us
    unnamed x4, waiting for transfers between devices  48 us
    all_gather x1, waiting for transfers between devices, local(): lax.all_gather(rows, 'tp', axis=2, tiled=True)  44.3 us
    unnamed x21, local copies, waits for them, and re-layouts  27.8 us
    all_to_all x1, waiting for transfers between devices, local(): lax.all_to_all(mid_rows, 'seq', split_axis=1, concat_axis=0, tiled=True)  25 us
    all_to_all x1, starting transfers between devices, local(): lax.all_to_all(mid_rows, 'seq', split_axis=1, concat_axis=0, tiled=True)  10.2 us
    all_to_all x2, local copies, waits for them, and re-layouts, local(): lax.all_to_all(mid_rows, 'seq', split_axis=1, concat_axis=0, tiled=True)  9.3 us
    unnamed x1, other arithmetic  8.73 us
  transfers between devices with their start and end apart: 4, of which 4 were waited for; matrix products, arithmetic and copies ran while one was open for 7% of the time, Pallas kernels for 0%

commit v1 on v0

v1 whole, which is shorter than its diff:
```python
import functools

import jax
import jax.numpy as jnp
from jax import lax
from jax.experimental import pallas as pl
from jax.experimental.pallas import tpu as pltpu
from jax.sharding import PartitionSpec as P

NORM_EPS = 1e-06
MESH = pl.DeviceIdType.MESH
BF16 = jnp.bfloat16
F32 = jnp.float32

NX, NZ, NY = 4, 8, 8
NSEQ = NX * NZ
FRAMES = 32
SPACE = 192
PLACES = SPACE // NSEQ
HALF = PLACES // 2
HD = 128
D = 3072
ROWS = HALF * FRAMES
FEAT = D // NY
SLICE = FEAT // 2
SLAB = 16
SCALE = HD**-0.5


def head_norm(values, gain):
    square_mean = jnp.mean(values * values, axis=-1, keepdims=True)
    return (values * lax.rsqrt(square_mean + NORM_EPS) * gain).astype(BF16)


def dot(a, b):
    return jnp.dot(a, b, preferred_element_type=F32)


def dot_t(a, b):
    return lax.dot_general(a, b, (((1,), (1,)), ((), ())), preferred_element_type=F32)


def one_hot(targets, columns):
    rows = targets.shape[0]
    return jnp.where(
        lax.broadcasted_iota(jnp.int32, (rows, columns), 1) == targets, 1.0, 0.0
    ).astype(BF16)


def row_iota(rows):
    return lax.broadcasted_iota(jnp.int32, (rows, 1), 0)


def kernel(
    tok_h, q_h, k_h, v_h, sgain_h, proj_h, sgate_h, shift_h, scale_h, w_h, tgain_h, proj2_h, tgate_h,
    out_ref,
    tok, q, k, v, sgain, proj, sgate, shift, scale, w, tgain, proj2, tgate,
    heads, slab_out, slab_in, pick, hv, hs, tokbuf, toksend, part_out, part_in, mid, th,
    part2_out, part2_in, osend, orecv,
    load_sem, wsend, wrecv, a_send, a_recv, x_send, x_recv, e1s, e1r, e2s, e2r, e3s, e3r,
):
    s = lax.axis_index("seq")
    t = lax.axis_index("tp")
    y = t // 2
    c = t % 2
    xx = s // NZ
    z = s % NZ
    sib = (s, t + 1 - 2 * c)

    def ydev(step):
        return (s, 2 * ((y + step) % NY) + c)

    def seq_peer(dx, dz):
        return ((xx + dx) % NX) * NZ + (z + dz) % NZ

    hops = sorted(
        [(dx, dz) for dx in range(NX) for dz in range(NZ) if dx or dz],
        key=lambda d: -(min(d[0], NX - d[0]) + min(d[1], NZ - d[1])),
    )

    def remote(src, dst, ss, rs, device):
        return pltpu.make_async_remote_copy(
            src_ref=src, dst_ref=dst, send_sem=ss, recv_sem=rs, device_id=device, device_id_type=MESH
        )

    own_cols = pl.multiple_of(c * (3 * HD), HD)
    rows_c = pl.multiple_of(c * HD, HD)
    loads = [
        (q_h.at[0], q), (k_h.at[0], k), (v_h.at[0], v), (sgain_h, sgain), (tok_h.at[0], tok),
        (proj_h, proj.at[pl.ds(rows_c, HD)]), (sgate_h, sgate),
        (scale_h, scale), (shift_h, shift), (tgain_h, tgain.at[c]),
        (w_h.at[0], w.at[:, pl.ds(own_cols, HD)]),
        (w_h.at[1], w.at[:, pl.ds(pl.multiple_of(own_cols + HD, HD), HD)]),
        (w_h.at[2], w.at[:, pl.ds(pl.multiple_of(own_cols + 2 * HD, HD), HD)]),
        (proj2_h, proj2.at[pl.ds(rows_c, HD)]), (tgate_h, tgate),
    ]
    loads = [pltpu.make_async_copy(a, b, load_sem.at[i]) for i, (a, b) in enumerate(loads)]
    for copy in loads:
        copy.start()

    barrier = pltpu.get_barrier_semaphore()
    for dx, dz in hops:
        pl.semaphore_signal(barrier, inc=1, device_id=(seq_peer(dx, dz), t), device_id_type=MESH)
    for step in range(1, NY):
        pl.semaphore_signal(barrier, inc=1, device_id=ydev(step), device_id_type=MESH)
    pl.semaphore_signal(barrier, inc=1, device_id=sib, device_id_type=MESH)

    for copy in loads[:4]:
        copy.wait()
    qn = head_norm(q[...].astype(F32), sgain[0])
    kn = head_norm(k[...].astype(F32), sgain[1])
    sc = dot_t(qn, kn) * SCALE
    ex = jnp.exp(sc - jnp.max(sc, axis=-1, keepdims=True))
    at = (ex / jnp.sum(ex, axis=-1, keepdims=True)).astype(BF16)
    heads[...] = dot(at, v[...]).astype(BF16)

    r = row_iota(NSEQ * SLAB)
    j, i = r // SLAB, r % SLAB
    loads[4].wait()
    tk = tok[...]
    col = lax.broadcasted_iota(jnp.int32, (SLICE, 2 * HD), 1)
    row = lax.broadcasted_iota(jnp.int32, (SLICE, 2 * HD), 0)
    rest = SLICE - HD
    spread = jnp.where(
        (row >= HD) & ((col == row - HD) | (col == row - HD + HD + rest)), 1.0, 0.0
    ).astype(BF16)
    tail = dot(tk, spread).astype(BF16)
    slab = dot(one_hot(jnp.where(i < PLACES, PLACES * j + i, -1), SPACE), heads[...])
    slab += dot(
        one_hot(jnp.where((i >= PLACES) & (i < 2 * PLACES), PLACES * j + i - PLACES, -1), SPACE), tk[:, :HD]
    )
    last = (i >= 2 * PLACES) & (i < 2 * PLACES + HALF)
    slab += dot(one_hot(jnp.where(last, PLACES * j + i - 2 * PLACES, -1), SPACE), tail[:, :HD])
    slab += dot(one_hot(jnp.where(last, PLACES * j + HALF + i - 2 * PLACES, -1), SPACE), tail[:, HD:])
    slab_out[...] = slab.astype(BF16).reshape(NSEQ, SLAB, HD)

    pl.semaphore_wait(barrier, len(hops) + NY)

    switch = [
        remote(slab_out.at[seq_peer(dx, dz)], slab_in.at[s], a_send.at[n], a_recv.at[n], (seq_peer(dx, dz), t))
        for n, (dx, dz) in enumerate(hops)
    ]
    for copy in switch:
        copy.start()
    slab_in[s] = slab_out[s]

    weights = [
        (proj_h, proj.at[pl.ds(rows_c, HD)]), (tgain_h, tgain.at[c]),
        (w_h.at[0], w.at[:, pl.ds(own_cols, HD)]),
        (w_h.at[1], w.at[:, pl.ds(pl.multiple_of(own_cols + HD, HD), HD)]),
        (w_h.at[2], w.at[:, pl.ds(pl.multiple_of(own_cols + 2 * HD, HD), HD)]),
        (proj2_h, proj2.at[pl.ds(rows_c, HD)]),
    ]
    weights = [remote(a, b, wsend.at[n], wrecv.at[n], sib) for n, (a, b) in enumerate(weights)]
    for copy in weights:
        copy.start()

    r = row_iota(ROWS)
    p, f = r // FRAMES, r % FRAMES
    pick[0] = one_hot(SLAB * f + HALF * c + p, NSEQ * SLAB)
    pick[1] = one_hot(SLAB * f + HALF * (1 - c) + p, NSEQ * SLAB)
    pick[2] = one_hot(SLAB * f + PLACES + HALF * c + p, NSEQ * SLAB)
    pick[3] = one_hot(SLAB * f + PLACES + HALF * (1 - c) + p, NSEQ * SLAB)
    pick[4] = one_hot(SLAB * f + 2 * PLACES + p, NSEQ * SLAB)

    for copy in switch:
        copy.wait_recv()
    got = slab_in[...].reshape(NSEQ * SLAB, HD)
    hs[...] = dot(pick[1], got).astype(BF16)
    swap_heads = remote(hs, hv.at[c], x_send.at[0], x_recv.at[0], sib)
    swap_heads.start()
    hv[c] = dot(pick[0], got).astype(BF16)
    toksend[:, :HD] = dot(pick[3], got).astype(BF16)
    third = dot(pick[4], got).astype(BF16)
    toksend[:, HD:] = third
    swap_tok = remote(toksend, tokbuf.at[c], x_send.at[1], x_recv.at[1], sib)
    swap_tok.start()
    tokbuf[c, :, :HD] = dot(pick[2], got).astype(BF16)
    tokbuf[c, :, HD:] = third

    def exchange(rows_a, rows_b, weight, buf_out, buf_in, ss, rs):
        copies = []
        for step in (4, 3, 5, 2, 6, 1, 7):
            cols = pl.ds(pl.multiple_of(((y + step) % NY) * FEAT, HD), FEAT)
            buf_out[step] = (dot(rows_a, weight[:HD, cols]) + dot(rows_b, weight[HD:, cols])).astype(BF16)
            copy = remote(buf_out.at[step], buf_in.at[step], ss.at[step], rs.at[step], ydev(step))
            copy.start()
            copies.append((step, copy))
        cols = pl.ds(pl.multiple_of(y * FEAT, HD), FEAT)
        return dot(rows_a, weight[:HD, cols]) + dot(rows_b, weight[HD:, cols]), copies

    def total_of(total, copies, buf_in):
        for step, copy in reversed(copies):
            copy.wait_recv()
            total = total + buf_in[step].astype(F32)
        return total

    loads[5].wait()
    weights[0].wait_recv()
    swap_heads.wait_recv()
    total, first = exchange(hv[0], hv[1], proj, part_out, part_in, e1s, e1r)

    swap_tok.wait_recv()
    lane = lax.broadcasted_iota(jnp.int32, (2 * HD, 1), 0)
    inner = lane - HD - rest * c
    base = jnp.where(lane < HD, lane, jnp.where((inner >= 0) & (inner < rest), HD + inner, -FEAT))
    own_tok = dot(tokbuf[0], one_hot(base, FEAT)) + dot(tokbuf[1], one_hot(base + SLICE, FEAT))

    loads[6].wait()
    cols_y = pl.ds(pl.multiple_of(y * FEAT, HD), FEAT)
    total = total_of(total, first, part_in)
    mid[y] = (own_tok + sgate[:, cols_y] * total).astype(BF16)

    gathers = []
    for step in (4, 3, 5, 2, 6, 1, 7):
        copy = remote(mid.at[y], mid.at[y], e2s.at[step], e2r.at[step], ydev(step))
        copy.start()
        gathers.append(copy)
    for copy in loads[7:]:
        copy.wait()
    for copy in weights[1:]:
        copy.wait_recv()
    for copy in gathers:
        copy.wait_recv()

    sums = jnp.zeros((ROWS, 1), F32)
    for n in range(NY):
        sums += jnp.sum(mid[n].astype(F32), axis=-1, keepdims=True)
    mean = sums * (1.0 / D)
    squares = jnp.zeros((ROWS, 1), F32)
    for n in range(NY):
        centre = mid[n].astype(F32) - mean
        squares += jnp.sum(centre * centre, axis=-1, keepdims=True)
    inv = lax.rsqrt(squares * (1.0 / D) + NORM_EPS)
    acc = jnp.zeros((ROWS, 6 * HD), F32)
    for n in range(NY):
        cols = slice(n * FEAT, (n + 1) * FEAT)
        modulated = ((mid[n].astype(F32) - mean) * inv * (1.0 + scale[:, cols]) + shift[:, cols]).astype(BF16)
        acc += dot(modulated, w[cols, :])

    same = (lax.broadcasted_iota(jnp.int32, (ROWS, ROWS), 0) // FRAMES) == (
        lax.broadcasted_iota(jnp.int32, (ROWS, ROWS), 1) // FRAMES
    )
    for n in range(2):
        part = acc[:, 3 * HD * n : 3 * HD * (n + 1)]
        qt = head_norm(part[:, :HD], tgain[n, 0])
        kt = head_norm(part[:, HD : 2 * HD], tgain[n, 1])
        vt = part[:, 2 * HD :].astype(BF16)
        st = jnp.where(same, dot_t(qt, kt) * SCALE, -1e30)
        et = jnp.where(same, jnp.exp(st - jnp.max(st, axis=-1, keepdims=True)), 0.0)
        att = (et / jnp.sum(et, axis=-1, keepdims=True)).astype(BF16)
        th[n] = dot(att, vt).astype(BF16)

    total, second = exchange(th[0], th[1], proj2, part2_out, part2_in, e3s, e3r)
    total = total_of(total, second, part2_in)
    out = (mid[y].astype(F32) + tgate[:, cols_y] * total).astype(BF16)

    feature = lax.broadcasted_iota(jnp.int32, (FEAT, SLICE), 0)
    column = lax.broadcasted_iota(jnp.int32, (FEAT, SLICE), 1)
    give = jnp.where(feature == column + SLICE * (1 - c), 1.0, 0.0).astype(BF16)
    keep = jnp.where(feature == column + SLICE * c, 1.0, 0.0).astype(BF16)
    osend[...] = dot(out, give).astype(BF16)
    swap_out = remote(osend, orecv, x_send.at[2], x_recv.at[2], sib)
    swap_out.start()
    out_ref[pl.ds(HALF * c, HALF)] = dot(out, keep).astype(BF16).reshape(HALF, FRAMES, SLICE)
    swap_out.wait_recv()
    out_ref[pl.ds(HALF * (1 - c), HALF)] = orecv[...].reshape(HALF, FRAMES, SLICE)

    for copy in switch + weights + gathers + [swap_heads, swap_tok, swap_out]:
        copy.wait_send()
    for step, copy in first + second:
        copy.wait_send()


def local(
    tokens, spatial_query, spatial_key, spatial_value, spatial_gain, spatial_proj, spatial_gate,
    temporal_shift, temporal_scale, temporal_weights, temporal_gain, temporal_proj, temporal_gate,
):
    vm = pltpu.VMEM
    dma = pltpu.SemaphoreType.DMA
    any_spec = pl.BlockSpec(memory_space=pltpu.HBM)
    out = pl.pallas_call(
        kernel,
        out_shape=jax.ShapeDtypeStruct((PLACES, FRAMES, SLICE), BF16),
        in_specs=[any_spec] * 13,
        out_specs=pl.BlockSpec(memory_space=pltpu.VMEM),
        scratch_shapes=[
            vm((SPACE, SLICE), BF16), vm((SPACE, HD), BF16), vm((SPACE, HD), BF16), vm((SPACE, HD), BF16),
            vm((2, 1, HD), F32), vm((2 * HD, D), BF16), vm((1, D), F32), vm((1, D), F32), vm((1, D), F32),
            vm((D, 6 * HD), BF16), vm((2, 2, 1, HD), F32), vm((2 * HD, D), BF16), vm((1, D), F32),
            vm((SPACE, HD), BF16),
            vm((NSEQ, SLAB, HD), BF16), vm((NSEQ, SLAB, HD), BF16),
            vm((5, ROWS, NSEQ * SLAB), BF16),
            vm((2, ROWS, HD), BF16), vm((ROWS, HD), BF16),
            vm((2, ROWS, 2 * HD), BF16), vm((ROWS, 2 * HD), BF16),
            vm((NY, ROWS, FEAT), BF16), vm((NY, ROWS, FEAT), BF16),
            vm((NY, ROWS, FEAT), BF16),
            vm((2, ROWS, HD), BF16),
            vm((NY, ROWS, FEAT), BF16), vm((NY, ROWS, FEAT), BF16),
            vm((ROWS, SLICE), BF16), vm((ROWS, SLICE), BF16),
            dma((15,)), dma((6,)), dma((6,)), dma((31,)), dma((31,)), dma((3,)), dma((3,)),
            dma((NY,)), dma((NY,)), dma((NY,)), dma((NY,)), dma((NY,)), dma((NY,)),
        ],
        compiler_params=pltpu.CompilerParams(
            collective_id=0, has_side_effects=True, vmem_limit_bytes=56 * 1024 * 1024
        ),
        name="spatial_temporal",
    )(
        tokens, spatial_query, spatial_key, spatial_value, spatial_gain, spatial_proj,
        spatial_gate.reshape(1, D), temporal_shift.reshape(1, D), temporal_scale.reshape(1, D),
        temporal_weights.transpose(1, 2, 0, 3).reshape(3, D, HD), temporal_gain, temporal_proj,
        temporal_gate.reshape(1, D),
    )
    return out.transpose(1, 0, 2)


def solution(mesh):
    placed = (
        P("seq", None, "tp"),
        P("seq", None, "tp"),
        P("seq", None, "tp"),
        P("seq", None, "tp"),
        P(None, "tp", None),
        P("tp", None),
        P(),
        P(),
        P(),
        P(None, "tp", None, None),
        P(None, "tp", None),
        P("tp", None),
        P(),
    )
    return jax.shard_map(
        local, mesh=mesh, in_specs=placed, out_specs=P(None, "seq", "tp"), check_vma=False
    )
```

time: 330 us -> 75.9 us (0.23)
  waiting for transfers between devices: 228 us -> 0 us
  Pallas kernels: 0 us -> 74.2 us
  local copies, waits for them, and re-layouts: 50.2 us -> 1.54 us
  other arithmetic: 15.9 us -> 0 us
  between operations: 13.3 us -> 0.01 us
  starting transfers between devices: 10.3 us -> 0 us
  matrix products: 10 us -> 0 us
    psum x1 -> x0, waiting for transfers between devices: 111 us -> none  [local(): lax.psum(terms.astype(jnp.bfloat16), 'tp').astype(jnp.float32)]
    pallas_call x0 -> x1, Pallas kernels: none -> 74.2 us  [local(): pl.pallas_call(kernel, out_shape=jax.ShapeDtypeStruct((PLACES, FRAMES, SL...]
    unnamed x4 -> x0, waiting for transfers between devices: 48 us -> none
    all_gather x1 -> x0, waiting for transfers between devices: 44.3 us -> none  [local(): lax.all_gather(rows, 'tp', axis=2, tiled=True)]
    unnamed x21 -> x1, local copies, waits for them, and re-layouts: 27.8 us -> 1.54 us
    all_to_all x1 -> x0, waiting for transfers between devices: 25 us -> none  [local(): lax.all_to_all(mid_rows, 'seq', split_axis=1, concat_axis=0, tiled=True)]
    all_to_all x1 -> x0, starting transfers between devices: 10.2 us -> none  [local(): lax.all_to_all(mid_rows, 'seq', split_axis=1, concat_axis=0, tiled=True)]
    dot_general x5 -> x0, matrix products: 10 us -> none  [the longest x1 3.36 us: temporal_inputs(): jnp.dot(normed.reshape(-1, model_width), temporal_weights.reshape(model_w...]
  transfers between devices with their start and end apart: 4 -> 0, of which waited for: 4 -> 0; matrix products, arithmetic and copies ran while one was open for 7% -> 0% of each run, Pallas kernels for 0% -> 0%
where the time goes in v1:
time: 75.9 us; the launch traced here: 75.8 us
  Pallas kernels  74.2 us (98%)
  local copies, waits for them, and re-layouts  1.54 us (2%)
    pallas_call x1, Pallas kernels, local(): pl.pallas_call(kernel, out_shape=jax.ShapeDtypeStruct((PLACES, FRAMES, SL...  74.2 us
    unnamed x1, local copies, waits for them, and re-layouts  1.54 us

profile of v1, /device:TPU:1, one launch (start us, length us, event | category | flops | bytes accessed | tf_op | source)
XLA Modules:
  0.0 75.8 jit_solution(12100400677302962125)
XLA Ops:
  0.0 74.2 %spatial_temporal.1 = bf16[6,32,192]{2,1,0:T(8,128)(2,1)} custom-call(bf16[1,192,192]{2,1,0:T(8,128)(2,1)} %tok_h.1, bf16[1,192,128]{2,1,0:T(8,128)(2,1)} %q_h.1, bf16[1,192,128]{2,1,0:T(8,128)(2,1)} %k_h.1, bf16[1,192,128]{2,1,0:T(8,128)(2,1)} %v_h.1, f32[2,1,128]{2,1,0:T(1,128)} %sgain_h.1, bf16[128,3072]{1,0:T(8,128)(2,1)} %proj_h.1, f32[1,3072]{1,0:T(1,128)} %bitcast.10, ...), custom_call_target="tpu_custom_call" | custom-call | tf_op jit(solution)/shard_map/spatial_temporal/pallas_call | solution.py:282
  74.3 1.5 %copy.15 = bf16[32,6,192]{2,0,1:T(8,128)(2,1)} copy(bf16[32,6,192]{2,0,1:T(8,128)(2,1)} %bitcast.9) | data formatting | bytes 147456

commit v2 on v1

--- a/solution.py
+++ b/solution.py
@@ -55,9 +55,9 @@
     tok_h, q_h, k_h, v_h, sgain_h, proj_h, sgate_h, shift_h, scale_h, w_h, tgain_h, proj2_h, tgate_h,
     out_ref,
     tok, q, k, v, sgain, proj, sgate, shift, scale, w, tgain, proj2, tgate,
-    heads, slab_out, slab_in, pick, hv, hs, tokbuf, toksend, part_out, part_in, mid, th,
+    heads, slab_out, slab_in, pick, hv, hs, tokbuf, toksend, part_out, part_in, mid, mod, th,
     part2_out, part2_in, osend, orecv,
-    load_sem, wsend, wrecv, a_send, a_recv, x_send, x_recv, e1s, e1r, e2s, e2r, e3s, e3r,
+    load_sem, wsend, wrecv, a_send, a_recv, x_send, x_recv, o_send, o_recv, e1s, e1r, e2s, e2r, e3s, e3r,
 ):
     s = lax.axis_index("seq")
     t = lax.axis_index("tp")
@@ -67,8 +67,10 @@
     z = s % NZ
     sib = (s, t + 1 - 2 * c)
 
+    sigma = 1 - 2 * c
+
     def ydev(step):
-        return (s, 2 * ((y + step) % NY) + c)
+        return (s, 2 * ((y + sigma * step + 2 * NY) % NY) + c)
 
     def seq_peer(dx, dz):
         return ((xx + dx) % NX) * NZ + (z + dz) % NZ
@@ -82,6 +84,17 @@
         return pltpu.make_async_remote_copy(
             src_ref=src, dst_ref=dst, send_sem=ss, recv_sem=rs, device_id=device, device_id_type=MESH
         )
+
+    sent, arrived = [], set()
+
+    def go(copy):
+        copy.start()
+        sent.append(copy)
+        return copy
+
+    def arrive(copy):
+        copy.wait_recv()
+        arrived.add(id(copy))
 
     own_cols = pl.multiple_of(c * (3 * HD), HD)
     rows_c = pl.multiple_of(c * HD, HD)
@@ -141,7 +154,7 @@
         for n, (dx, dz) in enumerate(hops)
     ]
     for copy in switch:
-        copy.start()
+        go(copy)
     slab_in[s] = slab_out[s]
 
     weights = [
@@ -153,7 +166,7 @@
     ]
     weights = [remote(a, b, wsend.at[n], wrecv.at[n], sib) for n, (a, b) in enumerate(weights)]
     for copy in weights:
-        copy.start()
+        go(copy)
 
     r = row_iota(ROWS)
     p, f = r // FRAMES, r % FRAMES
@@ -164,111 +177,157 @@
     pick[4] = one_hot(SLAB * f + 2 * PLACES + p, NSEQ * SLAB)
 
     for copy in switch:
-        copy.wait_recv()
+        arrive(copy)
     got = slab_in[...].reshape(NSEQ * SLAB, HD)
     hs[...] = dot(pick[1], got).astype(BF16)
-    swap_heads = remote(hs, hv.at[c], x_send.at[0], x_recv.at[0], sib)
-    swap_heads.start()
-    hv[c] = dot(pick[0], got).astype(BF16)
+    lanes_c = pl.ds(rows_c, HD)
+    swap_heads = remote(hs, hv.at[:, lanes_c], x_send.at[0], x_recv.at[0], sib)
+    go(swap_heads)
+    hv[:, lanes_c] = dot(pick[0], got).astype(BF16)
     toksend[:, :HD] = dot(pick[3], got).astype(BF16)
     third = dot(pick[4], got).astype(BF16)
     toksend[:, HD:] = third
     swap_tok = remote(toksend, tokbuf.at[c], x_send.at[1], x_recv.at[1], sib)
-    swap_tok.start()
+    go(swap_tok)
     tokbuf[c, :, :HD] = dot(pick[2], got).astype(BF16)
     tokbuf[c, :, HD:] = third
 
-    def exchange(rows_a, rows_b, weight, buf_out, buf_in, ss, rs):
-        copies = []
-        for step in (4, 3, 5, 2, 6, 1, 7):
-            cols = pl.ds(pl.multiple_of(((y + step) % NY) * FEAT, HD), FEAT)
-            buf_out[step] = (dot(rows_a, weight[:HD, cols]) + dot(rows_b, weight[HD:, cols])).astype(BF16)
-            copy = remote(buf_out.at[step], buf_in.at[step], ss.at[step], rs.at[step], ydev(step))
-            copy.start()
-            copies.append((step, copy))
-        cols = pl.ds(pl.multiple_of(y * FEAT, HD), FEAT)
-        return dot(rows_a, weight[:HD, cols]) + dot(rows_b, weight[HD:, cols]), copies
-
-    def total_of(total, copies, buf_in):
-        for step, copy in reversed(copies):
-            copy.wait_recv()
-            total = total + buf_in[step].astype(F32)
-        return total
+    def term(rows, weight, offset):
+        place = (y - sigma * offset + 2 * NY) % NY
+        return dot(rows, weight[:, pl.ds(pl.multiple_of(place * FEAT, HD), FEAT)])
+
+    def post(bufs, n, slot, step):
+        buf_out, buf_in, ss, rs = bufs
+        return go(remote(buf_out.at[n, slot], buf_in.at[n, slot], ss.at[n, slot], rs.at[n, slot], ydev(step)))
+
+    def fetch(bufs, n, slot, step):
+        buf_out, buf_in, ss, rs = bufs
+        arrive(remote(buf_out.at[n, slot], buf_in.at[n, slot], ss.at[n, slot], rs.at[n, slot], ydev(step)))
+        return buf_in[n, slot].astype(F32)
+
+    via = {4: -2, 3: -1, 5: 1, 1: -1, 7: 1, 2: -2, 6: 2}
+
+    def reduce_start(bufs, rows, weight, chunks):
+        for slot in (4, 3, 5, 1, 7):
+            value = term(rows, weight, slot).astype(BF16)
+            for at, n in enumerate(chunks):
+                bufs[0][n, slot] = value[at * FRAMES : (at + 1) * FRAMES]
+                post(bufs, n, slot, via[slot])
+        return [term(rows, weight, slot) for slot in (2, 6, 0)]
+
+    def reduce_forward(bufs, n, plus, minus):
+        bufs[0][n, 2] = (plus + fetch(bufs, n, 4, -2) + fetch(bufs, n, 3, -1)).astype(BF16)
+        post(bufs, n, 2, via[2])
+        bufs[0][n, 6] = (minus + fetch(bufs, n, 5, 1)).astype(BF16)
+        post(bufs, n, 6, via[6])
+
+    def reduce_end(bufs, n, own):
+        for slot in (1, 7, 2, 6):
+            own = own + fetch(bufs, n, slot, via[slot])
+        return own
+
+    first = (part_out, part_in, e1s, e1r)
+    second = (part2_out, part2_in, e3s, e3r)
 
     loads[5].wait()
-    weights[0].wait_recv()
-    swap_heads.wait_recv()
-    total, first = exchange(hv[0], hv[1], proj, part_out, part_in, e1s, e1r)
-
-    swap_tok.wait_recv()
+    arrive(weights[0])
+    arrive(swap_heads)
+    waiting = reduce_start(first, hv[...], proj, range(HALF))
+
+    arrive(swap_tok)
     lane = lax.broadcasted_iota(jnp.int32, (2 * HD, 1), 0)
     inner = lane - HD - rest * c
     base = jnp.where(lane < HD, lane, jnp.where((inner >= 0) & (inner < rest), HD + inner, -FEAT))
     own_tok = dot(tokbuf[0], one_hot(base, FEAT)) + dot(tokbuf[1], one_hot(base + SLICE, FEAT))
-
     loads[6].wait()
     cols_y = pl.ds(pl.multiple_of(y * FEAT, HD), FEAT)
-    total = total_of(total, first, part_in)
-    mid[y] = (own_tok + sgate[:, cols_y] * total).astype(BF16)
-
-    gathers = []
-    for step in (4, 3, 5, 2, 6, 1, 7):
-        copy = remote(mid.at[y], mid.at[y], e2s.at[step], e2r.at[step], ydev(step))
-        copy.start()
-        gathers.append(copy)
+    gate = sgate[:, cols_y]
+
+    def rows_of(values, n):
+        return values[n * FRAMES : (n + 1) * FRAMES]
+
+    for n in range(HALF):
+        reduce_forward(first, n, rows_of(waiting[0], n), rows_of(waiting[1], n))
+
+    def pass_on(n, offset, slot, step):
+        place = (y + sigma * offset + 2 * NY) % NY
+        return go(remote(mid.at[n, place], mid.at[n, place], e2s.at[n, slot], e2r.at[n, slot], ydev(step)))
+
+    def receive(n, offset):
+        place = (y + sigma * offset + 2 * NY) % NY
+        slot = offset % NY
+        arrive(remote(mid.at[n, place], mid.at[n, place], e2s.at[n, slot], e2r.at[n, slot], ydev(1)))
+
+    for n in range(HALF):
+        total = reduce_end(first, n, rows_of(waiting[2], n))
+        mid[n, y] = (rows_of(own_tok, n) + gate * total).astype(BF16)
+        pass_on(n, 0, 6, 2)
+        pass_on(n, 0, 2, -2)
+        pass_on(n, 0, 7, 1)
+        pass_on(n, 0, 1, -1)
+    for n in range(HALF):
+        receive(n, -2)
+        pass_on(n, -2, 4, 2)
+        pass_on(n, -2, 5, 1)
+        receive(n, 2)
+        pass_on(n, 2, 3, -1)
+
     for copy in loads[7:]:
         copy.wait()
     for copy in weights[1:]:
-        copy.wait_recv()
-    for copy in gathers:
-        copy.wait_recv()
-
-    sums = jnp.zeros((ROWS, 1), F32)
-    for n in range(NY):
-        sums += jnp.sum(mid[n].astype(F32), axis=-1, keepdims=True)
-    mean = sums * (1.0 / D)
-    squares = jnp.zeros((ROWS, 1), F32)
-    for n in range(NY):
-        centre = mid[n].astype(F32) - mean
-        squares += jnp.sum(centre * centre, axis=-1, keepdims=True)
-    inv = lax.rsqrt(squares * (1.0 / D) + NORM_EPS)
-    acc = jnp.zeros((ROWS, 6 * HD), F32)
-    for n in range(NY):
-        cols = slice(n * FEAT, (n + 1) * FEAT)
-        modulated = ((mid[n].astype(F32) - mean) * inv * (1.0 + scale[:, cols]) + shift[:, cols]).astype(BF16)
-        acc += dot(modulated, w[cols, :])
-
-    same = (lax.broadcasted_iota(jnp.int32, (ROWS, ROWS), 0) // FRAMES) == (
-        lax.broadcasted_iota(jnp.int32, (ROWS, ROWS), 1) // FRAMES
-    )
-    for n in range(2):
-        part = acc[:, 3 * HD * n : 3 * HD * (n + 1)]
-        qt = head_norm(part[:, :HD], tgain[n, 0])
-        kt = head_norm(part[:, HD : 2 * HD], tgain[n, 1])
-        vt = part[:, 2 * HD :].astype(BF16)
-        st = jnp.where(same, dot_t(qt, kt) * SCALE, -1e30)
-        et = jnp.where(same, jnp.exp(st - jnp.max(st, axis=-1, keepdims=True)), 0.0)
-        att = (et / jnp.sum(et, axis=-1, keepdims=True)).astype(BF16)
-        th[n] = dot(att, vt).astype(BF16)
-
-    total, second = exchange(th[0], th[1], proj2, part2_out, part2_in, e3s, e3r)
-    total = total_of(total, second, part2_in)
-    out = (mid[y].astype(F32) + tgate[:, cols_y] * total).astype(BF16)
-
+        arrive(copy)
+
+    def temporal(n):
+        sums = jnp.zeros((FRAMES, 1), F32)
+        for b in range(NY):
+            sums += jnp.sum(mid[n, b].astype(F32), axis=-1, keepdims=True)
+        mean = sums * (1.0 / D)
+        squares = jnp.zeros((FRAMES, 1), F32)
+        for b in range(NY):
+            centre = mid[n, b].astype(F32) - mean
+            squares += jnp.sum(centre * centre, axis=-1, keepdims=True)
+        inv = lax.rsqrt(squares * (1.0 / D) + NORM_EPS)
+        for b in range(NY):
+            cols = slice(b * FEAT, (b + 1) * FEAT)
+            mod[:, cols] = (
+                (mid[n, b].astype(F32) - mean) * inv * (1.0 + scale[:, cols]) + shift[:, cols]
+            ).astype(BF16)
+        acc = dot(mod[...], w[...])
+        for h in range(2):
+            part = acc[:, 3 * HD * h : 3 * HD * (h + 1)]
+            qt = head_norm(part[:, :HD], tgain[h, 0])
+            kt = head_norm(part[:, HD : 2 * HD], tgain[h, 1])
+            vt = part[:, 2 * HD :].astype(BF16)
+            st = dot_t(qt, kt) * SCALE
+            et = jnp.exp(st - jnp.max(st, axis=-1, keepdims=True))
+            att = (et / jnp.sum(et, axis=-1, keepdims=True)).astype(BF16)
+            th[n, :, h * HD : (h + 1) * HD] = dot(att, vt).astype(BF16)
+
+    waiting = []
+    for n in range(HALF):
+        for offset in (-1, 1, 3, -3, 4):
+            receive(n, offset)
+        temporal(n)
+        waiting.append(reduce_start(second, th[n], proj2, [n]))
+    for n in range(HALF):
+        reduce_forward(second, n, waiting[n][0], waiting[n][1])
+    gate = tgate[:, cols_y]
     feature = lax.broadcasted_iota(jnp.int32, (FEAT, SLICE), 0)
     column = lax.broadcasted_iota(jnp.int32, (FEAT, SLICE), 1)
     give = jnp.where(feature == column + SLICE * (1 - c), 1.0, 0.0).astype(BF16)
     keep = jnp.where(feature == column + SLICE * c, 1.0, 0.0).astype(BF16)
-    osend[...] = dot(out, give).astype(BF16)
-    swap_out = remote(osend, orecv, x_send.at[2], x_recv.at[2], sib)
-    swap_out.start()
-    out_ref[pl.ds(HALF * c, HALF)] = dot(out, keep).astype(BF16).reshape(HALF, FRAMES, SLICE)
-    swap_out.wait_recv()
-    out_ref[pl.ds(HALF * (1 - c), HALF)] = orecv[...].reshape(HALF, FRAMES, SLICE)
-
-    for copy in switch + weights + gathers + [swap_heads, swap_tok, swap_out]:
-        copy.wait_send()
-    for step, copy in first + second:
+    swaps = []
+    for n in range(HALF):
+        total = reduce_end(second, n, waiting[n][2])
+        out = (mid[n, y].astype(F32) + gate * total).astype(BF16)
+        osend[n] = dot(out, give).astype(BF16)
+        swaps.append(go(remote(osend.at[n], orecv.at[n], o_send.at[n], o_recv.at[n], sib)))
+        out_ref[HALF * c + n] = dot(out, keep).astype(BF16)
+    for n in range(HALF):
+        arrive(swaps[n])
+        out_ref[HALF * (1 - c) + n] = orecv[n]
+
+    for copy in sent:
         copy.wait_send()
 
 
@@ -278,6 +337,7 @@
 ):
     vm = pltpu.VMEM
     dma = pltpu.SemaphoreType.DMA
+    blocks = vm((HALF, NY, FRAMES, FEAT), BF16)
     any_spec = pl.BlockSpec(memory_space=pltpu.HBM)
     out = pl.pallas_call(
         kernel,
@@ -291,15 +351,16 @@
             vm((SPACE, HD), BF16),
             vm((NSEQ, SLAB, HD), BF16), vm((NSEQ, SLAB, HD), BF16),
             vm((5, ROWS, NSEQ * SLAB), BF16),
-            vm((2, ROWS, HD), BF16), vm((ROWS, HD), BF16),
+            vm((ROWS, 2 * HD), BF16), vm((ROWS, HD), BF16),
             vm((2, ROWS, 2 * HD), BF16), vm((ROWS, 2 * HD), BF16),
-            vm((NY, ROWS, FEAT), BF16), vm((NY, ROWS, FEAT), BF16),
-            vm((NY, ROWS, FEAT), BF16),
-            vm((2, ROWS, HD), BF16),
-            vm((NY, ROWS, FEAT), BF16), vm((NY, ROWS, FEAT), BF16),
-            vm((ROWS, SLICE), BF16), vm((ROWS, SLICE), BF16),
-            dma((15,)), dma((6,)), dma((6,)), dma((31,)), dma((31,)), dma((3,)), dma((3,)),
-            dma((NY,)), dma((NY,)), dma((NY,)), dma((NY,)), dma((NY,)), dma((NY,)),
+            blocks, blocks,
+            blocks, vm((FRAMES, D), BF16),
+            vm((HALF, FRAMES, 2 * HD), BF16),
+            blocks, blocks,
+            vm((HALF, FRAMES, SLICE), BF16), vm((HALF, FRAMES, SLICE), BF16),
+            dma((15,)), dma((6,)), dma((6,)), dma((31,)), dma((31,)), dma((2,)), dma((2,)),
+            dma((HALF,)), dma((HALF,)),
+            dma((HALF, NY)), dma((HALF, NY)), dma((HALF, NY)), dma((HALF, NY)), dma((HALF, NY)), dma((HALF, NY)),
         ],
         compiler_params=pltpu.CompilerParams(
             collective_id=0, has_side_effects=True, vmem_limit_bytes=56 * 1024 * 1024

time: 75.9 us -> 62.8 us (0.83)
  Pallas kernels: 74.2 us -> 61.1 us
    pallas_call x1, Pallas kernels: 74.2 us -> 61.1 us  [local(): pl.pallas_call(kernel, out_shape=jax.ShapeDtypeStruct((PLACES, FRAMES, SL...]
where the time goes in v2:
time: 62.8 us; the launch traced here: 62.7 us
  Pallas kernels  61.1 us (97%)
  local copies, waits for them, and re-layouts  1.54 us (2%)
    pallas_call x1, Pallas kernels, local(): pl.pallas_call(kernel, out_shape=jax.ShapeDtypeStruct((PLACES, FRAMES, SL...  61.1 us
    unnamed x1, local copies, waits for them, and re-layouts  1.54 us

profile of v2, /device:TPU:1, one launch (start us, length us, event | category | flops | bytes accessed | tf_op | source)
XLA Modules:
  0.0 62.7 jit_solution(10621306715476166858)
XLA Ops:
  0.0 61.1 %spatial_temporal.1 = bf16[6,32,192]{2,1,0:T(8,128)(2,1)} custom-call(bf16[1,192,192]{2,1,0:T(8,128)(2,1)} %tok_h.1, bf16[1,192,128]{2,1,0:T(8,128)(2,1)} %q_h.1, bf16[1,192,128]{2,1,0:T(8,128)(2,1)} %k_h.1, bf16[1,192,128]{2,1,0:T(8,128)(2,1)} %v_h.1, f32[2,1,128]{2,1,0:T(1,128)} %sgain_h.1, bf16[128,3072]{1,0:T(8,128)(2,1)} %proj_h.1, f32[1,3072]{1,0:T(1,128)} %bitcast.10, ...), custom_call_target="tpu_custom_call" | custom-call | tf_op jit(solution)/shard_map/spatial_temporal/pallas_call | solution.py:342
  61.1 1.5 %copy.15 = bf16[32,6,192]{2,0,1:T(8,128)(2,1)} copy(bf16[32,6,192]{2,0,1:T(8,128)(2,1)} %bitcast.9) | data formatting | bytes 147456
